TPU v7x, 256 devices: a whole 4x4x8 slice. The times are simulated.
256 devices in a mesh: pts: 64 (over z, x, core), snap: 4 (over y).
Axes of the slice: x: 4, y: 4, z: 8, core: 2. Of those that a mesh axis runs over, the one named last changes fastest.
Arguments:
- snapshots: float32 [262144, 1024], P('pts', 'snap'), may hold values from -6 to 6
- basis: float32 [262144, 128], P('pts'), may hold values from -0.01171875 to 0.01171875
- reg_linear: float32 [129], replicated, may hold values from 0.1 to 1
- reg_quadratic: float32 [8256], P('pts'), may hold values from 0.1 to 1
Outputs:
- coordinates: float32 [128, 1024], P(None, 'snap')
- gram_quad: float32 [8256, 8256], P('pts', 'snap')
- gram_cross: float32 [129, 8256], P(None, 'pts')
- gram_lin: float32 [129, 129], replicated
All inputs are finite; a program needn't handle non-finite values.
Results may differ from a plain program's by a relative error of at most 0.00017.
Values sent between devices are 32-bit elements; how exact they have to be, the bound alone decides.
A program may use at most 128 MiB of HBM per device.

v0:
```python
import jax
import jax.numpy as jnp
import numpy as np
from jax import lax
from jax.sharding import PartitionSpec as P

R = 128


def pair_table(width, slots):
    first, second = np.triu_indices(width)
    filled = first.shape[0]
    first_all = np.zeros((slots,), np.int32)
    second_all = np.zeros((slots,), np.int32)
    first_all[:filled] = first
    second_all[:filled] = second
    return np.stack([first_all, second_all], 0).astype(np.int32)


def pair_valid(width, slots):
    filled = width * (width + 1) // 2
    return (np.arange(slots) < filled).astype(np.float32)


def pair_rows(coords, pairs, valid):
    return jnp.take(coords, pairs[0], axis=0) * jnp.take(coords, pairs[1], axis=0) * valid[:, None]


def inner(left, right):
    return lax.dot_general(
        left,
        right,
        (((1,), (1,)), ((), ())),
        precision=lax.Precision.HIGHEST,
        preferred_element_type=jnp.float32,
    )


def shards(snapshots, basis, reg_linear, reg_quadratic):
    partial_proj = lax.dot_general(
        basis,
        snapshots,
        (((0,), (0,)), ((), ())),
        precision=lax.Precision.HIGHEST,
        preferred_element_type=jnp.float32,
    )
    group = lax.axis_index("snap")
    local_coords = lax.psum(partial_proj, "pts")
    every = lax.all_gather(local_coords, "snap", axis=1, tiled=True)
    total = every.shape[1]
    scale = 1.0 / total
    row_count = reg_quadratic.shape[0]
    quad_count = row_count * lax.axis_size("pts")
    table = jnp.asarray(pair_table(R, quad_count))
    valid = jnp.asarray(pair_valid(R, quad_count))
    row_start = lax.axis_index("pts") * row_count
    col_count = quad_count // lax.axis_size("snap")
    col_start = group * col_count
    row_feats = pair_rows(
        every,
        lax.dynamic_slice_in_dim(table, row_start, row_count, 1),
        lax.dynamic_slice_in_dim(valid, row_start, row_count, 0),
    )
    col_feats = pair_rows(
        every,
        lax.dynamic_slice_in_dim(table, col_start, col_count, 1),
        lax.dynamic_slice_in_dim(valid, col_start, col_count, 0),
    )
    block = inner(row_feats, col_feats)
    row_ids = row_start + jnp.arange(row_count, dtype=jnp.int32)
    col_ids = col_start + jnp.arange(col_count, dtype=jnp.int32)
    on_diag = row_ids[:, None] == col_ids[None, :]
    gram_quad = block * scale + jnp.where(on_diag, reg_quadratic[:, None], 0.0)
    linear = jnp.concatenate([every, jnp.ones((1, total), jnp.float32)], 0)
    gram_cross = inner(linear, row_feats) * scale
    gram_lin = inner(linear, linear) * scale + jnp.diag(reg_linear)
    return (local_coords, gram_quad, gram_cross, gram_lin)


def solution(mesh):
    placed = (P("pts", "snap"), P("pts", None), P(), P("pts"))
    return jax.shard_map(
        shards,
        mesh=mesh,
        in_specs=placed,
        out_specs=(P(None, "snap"), P("pts", "snap"), P(None, "pts"), P()),
        check_vma=False,
    )
```

profile of v0, /device:TPU:1, one launch (start us, length us, event | category | flops | bytes accessed | tf_op | source)
XLA Modules:
  0.0 249.4 jit_solution(12673909729170028690)
XLA Ops:
  7.2 0.0 copy-start
  7.2 0.0 copy-start.2
  7.2 0.0 all-reduce.3.cloned.1.call-start
  7.2 1.5 copy-done
  8.8 6.4 %fusion.13 = f32[128,256]{1,0:T(8,128)} fusion(f32[4096,128]{1,0:T(8,128)S(1)} %copy-done, f32[4096,256]{1,0:T(8,128)} %param.10), kind=kOutput, calls=%fused_computation.39 | convolution fusion | flops 1610612736 | bytes 6422528 | tf_op jit(solution)/shard_map/dot_general | solution.py:40
  15.1 0.0 all-reduce.3.cloned.1.call-update
  15.2 0.8 constant_dynamic-slice_fusion
  16.0 0.9 dynamic-slice_reduce_fusion.1
  17.1 175.3 %all-reduce.3.cloned.1.call-done = f32[128,256]{1,0:T(8,128)} async-done(((f32[128,256]{1,0:T(8,128)}), f32[128,256]{1,0:T(8,128)}) %all-reduce.3.cloned.1.call-update) | async-done | bytes 131088 | tf_op jit(solution)/shard_map/psum | solution.py:48
  192.4 12.4 %all_gather.3 = f32[128,1024]{1,0:T(8,128)S(1)} all-gather(f32[128,256]{1,0:T(8,128)} %all-reduce.3.cloned.1.call-done), channel_id=1, replica_groups=mesh['pts'=64,'snap'=4] {'snap'}, dimensions={1}, use_global_device_ids=true | all-gather | bytes 655360 | tf_op jit(solution)/shard_map/all_gather | solution.py:49
  204.8 0.0 copy-done.2
  204.8 1.3 fusion.7
  206.1 0.8 gather_fusion.1
  206.9 1.6 gather_fusion
  208.5 7.9 %gather_fusion.3 = f32[2064,1024]{1,0:T(8,128)} fusion(f32[128,1024]{1,0:T(8,128)S(1)} %all_gather.3, s32[3072]{0:T(1024)S(1)} %pad_clamp_fusion), kind=kCustom, calls=%fused_computation.3.clone | custom fusion | bytes 16916544 | tf_op jit(solution)/shard_map/jit(_take)/gather | solution.py:26
  216.4 0.0 copy-start.3
  216.4 8.0 %gather_fusion.2 = f32[2064,1024]{1,0:T(8,128)} fusion(f32[128,1024]{1,0:T(8,128)S(1)} %all_gather.3, s32[3072]{0:T(1024)S(1)} %pad_clamp_fusion.1), kind=kCustom, calls=%fused_computation.1.clone | custom fusion | bytes 16916544 | tf_op jit(solution)/shard_map/jit(_take)/gather | solution.py:26
  224.4 2.4 convolution_multiply_fusion.1
  226.9 0.0 copy-done.3
  226.9 0.0 copy-start.1
  226.9 15.0 %fusion.6 = f32[129,2064]{1,0:T(8,128)} fusion(f32[2064,1024]{1,0:T(8,128)} %gather_fusion.3, f32[2064,1024]{1,0:T(8,128)} %gather_fusion.2, pred[2064]{0:T(1024)(128)(4,1)S(1)} %get-tuple-element.12, pred[2064]{0:T(1024)(128)(4,1)S(1)} %get-tuple-element.13, f32[129]{0:T(256)S(1)} %copy-done.3, s32[2064]{0:T(1024)S(1)} %iota_add_fusion, ...), kind=kOutput, calls=%fused_computation.11 | convolution fusion | flops 3279555584 | bytes 19043754 | tf_op jit(solution)/shard_map/dot_general | solution.py:30
  241.9 0.0 copy-done.1
  241.9 0.7 copy.11
  (11 shorter events, 0.1 us)
Async XLA Ops:
  7.2 1.6 copy-start
  7.2 197.6 %copy-start.2 = (f32[129]{0:T(256)S(1)}, f32[129]{0:T(256)}, u32[]{:S(2)}) copy-start(f32[129]{0:T(256)} %param.12) | copy-start | bytes 1552
  7.2 185.2 %all-reduce.3.cloned.1.call-start = ((), (), s32[]{:S(2)}) async-start(), calls=%async_computation | async-start | bytes 262144 | tf_op jit(solution)/shard_map/psum | solution.py:48
  216.4 10.5 %copy-start.3 = (f32[129]{0:T(256)S(1)}, f32[129]{0:T(256)}, u32[]{:S(2)}) copy-start(f32[129]{0:T(256)} %param.13) | copy-start | bytes 1552
  226.9 15.0 %copy-start.1 = (f32[128,256]{1,0:T(8,128)S(1)}, f32[128,256]{1,0:T(8,128)}, u32[]{:S(2)}) copy-start(f32[128,256]{1,0:T(8,128)} %all-reduce.3.cloned.1.call-done) | copy-start | bytes 393220
Sparse Core Ops, SparseCore 0:
  15.3 177.0 all-reduce.2
where the time goes:
time: 250 us; the launch traced here: 249 us
  waiting for transfers between devices  175 us (70%)
  matrix products  25.1 us (10%)
  local copies, waits for them, and re-layouts  22.3 us (9%)
  between operations  14.1 us (6%)
  blocking collectives  12.4 us (5%)
    psum x1, waiting for transfers between devices, shards(): local_coords = lax.psum(partial_proj, 'pts')  175 us
    dot_general x3, matrix products, inner(): lax.dot_general(left, right, (((1,), (1,)), ((), ())), precision=lax.Prec...  18.7 us
    all_gather x1, blocking collectives, shards(): every = lax.all_gather(local_coords, 'snap', axis=1, tiled=True)  12.4 us
    gather x2, local copies, waits for them, and re-layouts, pair_rows(): jnp.take(coords, pairs[0], axis=0) * jnp.take(coords, pairs[1], axis=0)  9.63 us
    gather x2, local copies, waits for them, and re-layouts, pair_rows(): jnp.take(coords, pairs[1], axis=0)  8.7 us
    dot_general x1, matrix products, shards(): lax.dot_general(basis, snapshots, (((0,), (0,)), ((), ())), precision=lax...  6.37 us
  transfers between devices with their start and end apart: 1, of which 1 were waited for; matrix products, arithmetic and copies ran while one was open for 1% of the time, Pallas kernels for 0%

commit v1 on v0

v1 whole, which is shorter than its diff:
```python
import functools

import jax
import jax.numpy as jnp
import numpy as np
from jax import lax
from jax.experimental import pallas as pl
from jax.experimental.pallas import tpu as pltpu
from jax.sharding import PartitionSpec as P

R = 128
MESH = pl.DeviceIdType.MESH
CHUNKS = 8
NZ, NX, NC, NY = 8, 4, 2, 4
XY = [(dx, dy) for dy in range(NY) for dx in range(NX) if dx or dy]


def split(value):
    high = value.astype(jnp.bfloat16)
    low = (value - high.astype(jnp.float32)).astype(jnp.bfloat16)
    return high, low


def dot_rows(left, right):
    return lax.dot_general(left, right, (((0,), (0,)), ((), ())), preferred_element_type=jnp.float32)


def gather_kernel(basis_hbm, snaps_hbm, out_hbm, basis, snaps, part, peer, half, from_x, from_z, full,
                  in_sem, c_send, c_recv, x_send, x_recv, z_send, z_recv, xy_send, xy_recv, f_send, f_recv, out_sem):
    pts, y = lax.axis_index("pts"), lax.axis_index("snap")
    z, x, c = pts // (NX * NC), (pts // NC) % NX, pts % NC

    def device(z_of, x_of, c_of, y_of):
        return ((z_of * NX + x_of) * NC + c_of, y_of)

    sibling = device(z, x, 1 - c, y)
    x_peers = [device(z, (x + k) % NX, c, y) for k in range(1, NX)]
    z_peers = [device((z + k) % NZ, x, c, y) for k in range(1, NZ)]
    xy_peers = [device(z, (x + dx) % NX, c, (y + dy) % NY) for dx, dy in XY]

    barrier = pltpu.get_barrier_semaphore()
    greeted = [sibling] + z_peers + xy_peers
    for peer_id in greeted:
        pl.semaphore_signal(barrier, inc=1, device_id=peer_id, device_id_type=MESH)

    rows = basis.shape[1]
    loads = []
    for k in range(CHUNKS):
        for j, (src, dst) in enumerate(((basis_hbm, basis), (snaps_hbm, snaps))):
            load = pltpu.make_async_copy(src.at[pl.ds(k * rows, rows)], dst.at[k], in_sem.at[k, j])
            load.start()
            loads.append(load)
    for k in range(CHUNKS):
        loads[2 * k].wait()
        loads[2 * k + 1].wait()
        b_high, b_low = split(basis[k])
        s_high, s_low = split(snaps[k])
        both = dot_rows(jnp.concatenate([b_high, b_low], axis=1), s_high)
        term = both[:R] + both[R:] + dot_rows(b_high, s_low)
        for h in range(NC):
            if k == 0:
                part[h] = term[:, h * R:(h + 1) * R]
            else:
                part[h] += term[:, h * R:(h + 1) * R]
    pl.semaphore_wait(barrier, len(greeted))

    copy = pltpu.make_async_remote_copy(part.at[1 - c], peer, c_send, c_recv, device_id=sibling, device_id_type=MESH)
    copy.start()
    copy.wait()
    half[...] = (part[c] + peer[...]).reshape(half.shape)

    copies = []
    for k in range(1, NX):
        copy = pltpu.make_async_remote_copy(half.at[(x + k) % NX], from_x.at[k - 1], x_send.at[k - 1], x_recv.at[k - 1],
                                            device_id=x_peers[k - 1], device_id_type=MESH)
        copy.start()
        copies.append(copy)
    for copy in copies:
        copy.wait()
    from_z[z] = half[x] + from_x[0] + from_x[1] + from_x[2]

    copies = []
    for k in range(1, NZ):
        copy = pltpu.make_async_remote_copy(from_z.at[z], from_z.at[z], z_send.at[k - 1], z_recv.at[k - 1],
                                            device_id=z_peers[k - 1], device_id_type=MESH)
        copy.start()
        copies.append(copy)
    for copy in copies:
        copy.wait()
    total = from_z[0]
    for k in range(1, NZ):
        total += from_z[k]
    full[2 * y + c, x] = total

    copies = []
    for n, peer_id in enumerate(xy_peers):
        copy = pltpu.make_async_remote_copy(full.at[2 * y + c, x], full.at[2 * y + c, x], xy_send.at[n], xy_recv.at[n],
                                            device_id=peer_id, device_id_type=MESH)
        copy.start()
        copies.append(copy)
    handed = []
    for dy in range(NY):
        for n, (_, step) in enumerate(XY):
            if step == dy:
                copies[n].wait_recv()
        y_from = (y - dy + NY) % NY
        copy = pltpu.make_async_remote_copy(full.at[2 * y_from + c], full.at[2 * y_from + c], f_send.at[dy], f_recv.at[dy],
                                            device_id=sibling, device_id_type=MESH)
        copy.start()
        handed.append(copy)
    for copy in handed:
        copy.wait_recv()
    copy = pltpu.make_async_copy(full, out_hbm, out_sem)
    copy.start()
    for copy_out in copies + handed:
        copy_out.wait_send()
    copy.wait()


def gather_call(basis, snapshots):
    points, width = snapshots.shape
    rows = points // CHUNKS
    dma = pltpu.SemaphoreType.DMA
    block = (NX, R // NX, R)
    return pl.pallas_call(
        gather_kernel,
        out_shape=jax.ShapeDtypeStruct((NC * NY,) + block, jnp.float32),
        in_specs=[pl.BlockSpec(memory_space=pl.ANY)] * 2,
        out_specs=pl.BlockSpec(memory_space=pl.ANY),
        scratch_shapes=[
            pltpu.VMEM((CHUNKS, rows, R), jnp.float32),
            pltpu.VMEM((CHUNKS, rows, width), jnp.float32),
            pltpu.VMEM((NC, R, R), jnp.float32),
            pltpu.VMEM((R, R), jnp.float32),
            pltpu.VMEM(block, jnp.float32),
            pltpu.VMEM((NX - 1,) + block[1:], jnp.float32),
            pltpu.VMEM((NZ,) + block[1:], jnp.float32),
            pltpu.VMEM((NC * NY,) + block, jnp.float32),
            dma((CHUNKS, 2)),
            dma, dma,
            dma((NX - 1,)), dma((NX - 1,)),
            dma((NZ - 1,)), dma((NZ - 1,)),
            dma((len(XY),)), dma((len(XY),)),
            dma((NY,)), dma((NY,)),
            dma,
        ],
        compiler_params=pltpu.CompilerParams(collective_id=0, has_side_effects=True, vmem_limit_bytes=48 << 20),
        name="project_and_gather",
    )(basis, snapshots)


def pair_table(width):
    return np.stack(np.triu_indices(width), 0).astype(np.int32)


def pair_rows(coords, pairs):
    return jnp.take(coords, pairs[0], axis=0) * jnp.take(coords, pairs[1], axis=0)


def inner(left, right):
    return lax.dot_general(left, right, (((1,), (1,)), ((), ())), precision=lax.Precision.HIGH,
                           preferred_element_type=jnp.float32)


def shards(snapshots, basis, reg_linear, reg_quadratic):
    blocks = gather_call(basis, snapshots).reshape(NC * NY, R, R)
    every = blocks.transpose(1, 0, 2).reshape(R, NC * NY * R)
    group = lax.axis_index("snap")
    local_coords = lax.dynamic_slice_in_dim(every, group * NC * R, NC * R, 1)
    total = every.shape[1]
    scale = 1.0 / total
    row_count = reg_quadratic.shape[0]
    quad_count = row_count * lax.axis_size("pts")
    table = jnp.asarray(pair_table(R))
    row_start = lax.axis_index("pts") * row_count
    col_count = quad_count // lax.axis_size("snap")
    col_start = group * col_count
    row_feats = pair_rows(every, lax.dynamic_slice_in_dim(table, row_start, row_count, 1))
    col_feats = pair_rows(every, lax.dynamic_slice_in_dim(table, col_start, col_count, 1))
    block = inner(row_feats, col_feats)
    row_ids = row_start + jnp.arange(row_count, dtype=jnp.int32)
    col_ids = col_start + jnp.arange(col_count, dtype=jnp.int32)
    on_diag = row_ids[:, None] == col_ids[None, :]
    gram_quad = block * scale + jnp.where(on_diag, reg_quadratic[:, None], 0.0)
    linear = jnp.concatenate([every, jnp.ones((1, total), jnp.float32)], 0)
    gram_cross = inner(linear, row_feats) * scale
    gram_lin = inner(linear, linear) * scale + jnp.diag(reg_linear)
    return (local_coords, gram_quad, gram_cross, gram_lin)


def solution(mesh):
    placed = (P("pts", "snap"), P("pts", None), P(), P("pts"))
    return jax.shard_map(
        shards,
        mesh=mesh,
        in_specs=placed,
        out_specs=(P(None, "snap"), P("pts", "snap"), P(None, "pts"), P()),
        check_vma=False,
    )
```

time: 250 us -> 65.4 us (0.26)
  waiting for transfers between devices: 175 us -> 0 us
  Pallas kernels: 0 us -> 29.1 us
  between operations: 14.1 us -> 0.75 us
  blocking collectives: 12.4 us -> 0 us
  matrix products: 25.1 us -> 13.5 us
    psum x1 -> x0, waiting for transfers between devices: 175 us -> none  [shards(): local_coords = lax.psum(partial_proj, 'pts')]
    pallas_call x0 -> x1, Pallas kernels: none -> 29.1 us  [gather_call(): pl.pallas_call(gather_kernel, out_shape=jax.ShapeDtypeStruct((NC * NY,) +...]
    all_gather x1 -> x0, blocking collectives: 12.4 us -> none  [shards(): every = lax.all_gather(local_coords, 'snap', axis=1, tiled=True)]
    dot_general x1 -> x0, matrix products: 6.37 us -> none  [shards(): lax.dot_general(basis, snapshots, (((0,), (0,)), ((), ())), precision=lax...]
    dot_general x3, matrix products: 18.7 us -> 13.5 us  [inner(): lax.dot_general(left, right, (((1,), (1,)), ((), ())), precision=lax.Prec...]
  transfers between devices with their start and end apart: 1 -> 0, of which waited for: 1 -> 0; matrix products, arithmetic and copies ran while one was open for 1% -> 0% of each run, Pallas kernels for 0% -> 0%
where the time goes in v1:
time: 65.4 us; the launch traced here: 65.2 us
  Pallas kernels  29.1 us (44%)
  local copies, waits for them, and re-layouts  21.7 us (33%)
  matrix products  13.5 us (21%)
  between operations  0.75 us (1%)
    pallas_call x1, Pallas kernels, gather_call(): pl.pallas_call(gather_kernel, out_shape=jax.ShapeDtypeStruct((NC * NY,) +...  29.1 us
    dot_general x3, matrix products, inner(): lax.dot_general(left, right, (((1,), (1,)), ((), ())), precision=lax.Prec...  13.5 us
    gather x2, local copies, waits for them, and re-layouts, pair_rows(): jnp.take(coords, pairs[0], axis=0) * jnp.take(coords, pairs[1], axis=0)  8.86 us
    gather x2, local copies, waits for them, and re-layouts, pair_rows(): jnp.take(coords, pairs[1], axis=0)  8.73 us
    slice x2, local copies, waits for them, and re-layouts, pair_rows(): pairs[0]  1.76 us
    unnamed x4, local copies, waits for them, and re-layouts  1.59 us

profile of v1, /device:TPU:1, one launch (start us, length us, event | category | flops | bytes accessed | tf_op | source)
XLA Modules:
  0.0 65.2 jit_solution(279327417201502949)
XLA Ops:
  0.6 0.8 %constant_dynamic-slice_fusion = (s32[1,129]{1,0:T(1,128)S(1)}, s32[1,129]{1,0:T(1,128)S(1)}) fusion(s32[2,8256]{1,0:T(2,128)} %constant.27.clone, s32[]{:T(128)S(6)} %select_n.33, s32[]{:T(128)S(6)} %add.72), kind=kLoop, calls=%fused_computation.36 | loop fusion | bytes 2072 | tf_op jit(solution)/shard_map/slice | solution.py:157
  1.6 0.9 %dynamic-slice_reduce_fusion.1 = (s32[2064]{0:T(1024)S(1)}, s32[2064]{0:T(1024)S(1)}) fusion(s32[2,8256]{1,0:T(2,128)} %constant.27.clone, s32[]{:T(128)S(6)} %select_n.34, s32[]{:T(128)S(6)} %add.72), kind=kLoop, calls=%fused_computation.28 | loop fusion | bytes 33032 | tf_op jit(solution)/shard_map/slice | solution.py:157
  2.5 0.0 copy-start
  2.6 1.6 %copy-done = f32[4096,128]{1,0:T(8,128)S(1)} copy-done((f32[4096,128]{1,0:T(8,128)S(1)}, f32[4096,128]{1,0:T(8,128)}, u32[]{:S(2)}) %copy-start) | copy-done | bytes 2097176
  4.1 29.1 %project_and_gather.1 = f32[8,4,32,128]{3,2,1,0:T(8,128)S(1)} custom-call(f32[4096,128]{1,0:T(8,128)S(1)} %copy-done, f32[4096,256]{1,0:T(8,128)} %snaps_hbm.1), custom_call_target="tpu_custom_call" | custom-call | tf_op jit(solution)/shard_map/project_and_gather/pallas_call | solution.py:125
  33.3 0.7 %constant_dynamic-slice_fusion.1 = f32[128,256]{1,0:T(8,128)} fusion(f32[128,1024]{1,0:T(8,128)S(1)} %bitcast.10, s32[]{:T(128)S(6)} %select_n.32), kind=kLoop, calls=%fused_computation.37 | loop fusion | bytes 262148 | tf_op jit(solution)/shard_map/dynamic_slice | solution.py:169
  34.0 1.7 %fusion.7 = f32[129,129]{1,0:T(8,128)} fusion(f32[128,1024]{1,0:T(8,128)S(1)} %bitcast.11, f32[129]{0:T(256)} %param.11), kind=kOutput, calls=%fused_computation.14 | convolution fusion | flops 102308864 | bytes 591368 | tf_op jit(solution)/shard_map/dot_general | solution.py:161
  35.7 0.8 %gather_fusion.1 = f32[129,1024]{1,0:T(8,128)S(1)} fusion(f32[128,1024]{1,0:T(8,128)S(1)} %bitcast.12, s32[1024]{0:T(1024)S(1)} %pad_clamp_fusion.2), kind=kCustom, calls=%fused_computation.2.clone | custom fusion | bytes 1057284 | tf_op jit(solution)/shard_map/jit(_take)/gather | solution.py:157
  36.6 0.8 %gather_fusion = f32[129,1024]{1,0:T(8,128)S(1)} fusion(f32[128,1024]{1,0:T(8,128)S(1)} %bitcast.13, s32[1024]{0:T(1024)S(1)} %pad_clamp_fusion.3), kind=kCustom, calls=%fused_computation.clone | custom fusion | bytes 1057284 | tf_op jit(solution)/shard_map/jit(_take)/gather | solution.py:157
  37.4 1.2 %convolution_multiply_fusion.1 = f32[129,129]{1,0:T(8,128)} fusion(f32[128,1024]{1,0:T(8,128)S(1)} %bitcast.14, f32[129,1024]{1,0:T(8,128)S(1)} %gather_fusion.1, f32[129,1024]{1,0:T(8,128)S(1)} %gather_fusion, pred[129]{0:T(512)(128)(4,1)S(1)} %get-tuple-element.12, pred[129]{0:T(512)(128)(4,1)S(1)} %get-tuple-element.13), kind=kOutput, calls=%fused_computation.13 | convolution fusion | flops 102655232 | bytes 1647878 | tf_op jit(solution)/shard_map/dot_general | solution.py:161
  38.5 7.9 %gather_fusion.3 = f32[2064,1024]{1,0:T(8,128)} fusion(f32[128,1024]{1,0:T(8,128)S(1)} %bitcast.15, s32[3072]{0:T(1024)S(1)} %pad_clamp_fusion), kind=kCustom, calls=%fused_computation.3.clone | custom fusion | bytes 16916544 | tf_op jit(solution)/shard_map/jit(_take)/gather | solution.py:157
  46.5 0.0 copy-start.1
  46.5 8.0 %gather_fusion.2 = f32[2064,1024]{1,0:T(8,128)} fusion(f32[128,1024]{1,0:T(8,128)S(1)} %bitcast.16, s32[3072]{0:T(1024)S(1)} %pad_clamp_fusion.1), kind=kCustom, calls=%fused_computation.1.clone | custom fusion | bytes 16916544 | tf_op jit(solution)/shard_map/jit(_take)/gather | solution.py:157
  54.5 0.0 copy-done.1
  54.5 10.7 %fusion.6 = f32[129,2064]{1,0:T(8,128)} fusion(f32[2064,1024]{1,0:T(8,128)} %gather_fusion.3, f32[2064,1024]{1,0:T(8,128)} %gather_fusion.2, pred[2064]{0:T(1024)(128)(4,1)S(1)} %get-tuple-element.16, pred[2064]{0:T(1024)(128)(4,1)S(1)} %get-tuple-element.17, f32[129]{0:T(256)S(1)} %copy-done.1, s32[2064]{0:T(1024)S(1)} %iota_add_fusion, ...), kind=kOutput, calls=%fused_computation.11 | convolution fusion | flops 1643678720 | bytes 19043754 | tf_op jit(solution)/shard_map/dot_general | solution.py:161
  (11 shorter events, 0.1 us)
Async XLA Ops:
  2.5 1.6 %copy-start = (f32[4096,128]{1,0:T(8,128)S(1)}, f32[4096,128]{1,0:T(8,128)}, u32[]{:S(2)}) copy-start(f32[4096,128]{1,0:T(8,128)} %basis_hbm.1) | copy-start | bytes 6291460
  46.5 8.0 %copy-start.1 = (f32[129]{0:T(256)S(1)}, f32[129]{0:T(256)}, u32[]{:S(2)}) copy-start(f32[129]{0:T(256)} %param.12) | copy-start | bytes 1552

commit v2 on v1

--- a/solution.py
+++ b/solution.py
@@ -2,7 +2,6 @@
 
 import jax
 import jax.numpy as jnp
-import numpy as np
 from jax import lax
 from jax.experimental import pallas as pl
 from jax.experimental.pallas import tpu as pltpu
@@ -11,6 +10,8 @@
 R = 128
 MESH = pl.DeviceIdType.MESH
 CHUNKS = 8
+STEP = 16
+TILE = 256
 NZ, NX, NC, NY = 8, 4, 2, 4
 XY = [(dx, dy) for dy in range(NY) for dx in range(NX) if dx or dy]
 
@@ -44,6 +45,7 @@
         pl.semaphore_signal(barrier, inc=1, device_id=peer_id, device_id_type=MESH)
 
     rows = basis.shape[1]
+    quarter = half.shape[1]
     loads = []
     for k in range(CHUNKS):
         for j, (src, dst) in enumerate(((basis_hbm, basis), (snaps_hbm, snaps))):
@@ -90,11 +92,12 @@
     total = from_z[0]
     for k in range(1, NZ):
         total += from_z[k]
-    full[2 * y + c, x] = total
+    mine = full.at[2 * y + c, pl.ds(pl.multiple_of(x * quarter, quarter), quarter)]
+    mine[...] = total
 
     copies = []
     for n, peer_id in enumerate(xy_peers):
-        copy = pltpu.make_async_remote_copy(full.at[2 * y + c, x], full.at[2 * y + c, x], xy_send.at[n], xy_recv.at[n],
+        copy = pltpu.make_async_remote_copy(mine, mine, xy_send.at[n], xy_recv.at[n],
                                             device_id=peer_id, device_id_type=MESH)
         copy.start()
         copies.append(copy)
@@ -110,7 +113,7 @@
         handed.append(copy)
     for copy in handed:
         copy.wait_recv()
-    copy = pltpu.make_async_copy(full, out_hbm, out_sem)
+    copy = pltpu.make_async_copy(full, out_hbm.at[:, pl.ds(0, R)], out_sem)
     copy.start()
     for copy_out in copies + handed:
         copy_out.wait_send()
@@ -124,7 +127,7 @@
     block = (NX, R // NX, R)
     return pl.pallas_call(
         gather_kernel,
-        out_shape=jax.ShapeDtypeStruct((NC * NY,) + block, jnp.float32),
+        out_shape=jax.ShapeDtypeStruct((NC * NY, R + STEP, R), jnp.float32),
         in_specs=[pl.BlockSpec(memory_space=pl.ANY)] * 2,
         out_specs=pl.BlockSpec(memory_space=pl.ANY),
         scratch_shapes=[
@@ -135,7 +138,7 @@
             pltpu.VMEM(block, jnp.float32),
             pltpu.VMEM((NX - 1,) + block[1:], jnp.float32),
             pltpu.VMEM((NZ,) + block[1:], jnp.float32),
-            pltpu.VMEM((NC * NY,) + block, jnp.float32),
+            pltpu.VMEM((NC * NY, R, R), jnp.float32),
             dma((CHUNKS, 2)),
             dma, dma,
             dma((NX - 1,)), dma((NX - 1,)),
@@ -149,43 +152,132 @@
     )(basis, snapshots)
 
 
-def pair_table(width):
-    return np.stack(np.triu_indices(width), 0).astype(np.int32)
-
-
-def pair_rows(coords, pairs):
-    return jnp.take(coords, pairs[0], axis=0) * jnp.take(coords, pairs[1], axis=0)
-
-
-def inner(left, right):
-    return lax.dot_general(left, right, (((1,), (1,)), ((), ())), precision=lax.Precision.HIGH,
-                           preferred_element_type=jnp.float32)
+def first_index(pair):
+    found = jnp.int32(0)
+    for step in (64, 32, 16, 8, 4, 2, 1):
+        tried = found + step
+        found = jnp.where(pairs_before(tried) <= pair, tried, found)
+    return found
+
+
+def pairs_before(i):
+    return R * i - i * (i - 1) // 2
+
+
+def build_features(coords, feats, start, count):
+    first, last = first_index(start), first_index(start + count - 1)
+
+    @pl.loop(first, last + 1)
+    def _(i):
+        begun = pairs_before(i)
+        into = jnp.maximum(begun - start, 0)
+        j = i + jnp.maximum(start - begun, 0)
+        length = jnp.minimum(R - j, count - into)
+        base = coords[:, pl.ds(i, 1), :]
+
+        @pl.loop(0, (length + STEP - 1) // STEP)
+        def _(m):
+            feats[:, pl.ds(into + m * STEP, STEP), :] = base * coords[:, pl.ds(j + m * STEP, STEP), :]
+
+
+def lanes(blocks):
+    return jnp.concatenate([blocks[t] for t in range(blocks.shape[0])], axis=1)
+
+
+def gram_kernel(coords, reg_lin, reg_quad, local_out, quad_out, cross_out, lin_out, row_feats, col_feats, rows_split, lin_split):
+    pts, y = lax.axis_index("pts"), lax.axis_index("snap")
+    row_count, col_count = quad_out.shape
+    padded = rows_split.shape[1]
+    total = rows_split.shape[2]
+    scale = 1.0 / total
+    row_start, col_start = pts * row_count, y * col_count
+    for h in range(NC):
+        local_out[:, h * R:(h + 1) * R] = coords[NC * y + h, :R, :]
+    build_features(coords, row_feats, row_start, row_count)
+    build_features(coords, col_feats, col_start, col_count)
+
+    for t in range(coords.shape[0]):
+        high, low = split(row_feats[t, :padded, :])
+        rows_split[0, :, t * R:(t + 1) * R] = high
+        rows_split[1, :, t * R:(t + 1) * R] = low
+        extra = jnp.where(lax.broadcasted_iota(jnp.int32, (padded - R, R), 0) == 0, 1.0, 0.0)
+        high, low = split(jnp.concatenate([coords[t, :R, :], extra], axis=0))
+        lin_split[0, :, t * R:(t + 1) * R] = high
+        lin_split[1, :, t * R:(t + 1) * R] = low
+
+    def product(left, right_high, right_low):
+        dims = (((1,), (1,)), ((), ()))
+        both = lax.dot_general(left[...].reshape(2 * padded, total), right_high, dims, preferred_element_type=jnp.float32)
+        return both[:padded] + both[padded:] + lax.dot_general(left[0], right_low, dims, preferred_element_type=jnp.float32)
+
+    def regs_down(reg):
+        shape = (padded, reg.shape[1])
+        on = lax.broadcasted_iota(jnp.int32, shape, 0) == lax.broadcasted_iota(jnp.int32, shape, 1)
+        return on, jnp.sum(jnp.where(on, jnp.broadcast_to(reg[...], shape), 0.0), axis=1, keepdims=True)
+
+    on, reg_column = regs_down(reg_lin)
+    size = lin_out.shape[0]
+    cross_out[...] = (product(lin_split, rows_split[0], rows_split[1]) * scale)[:size, :row_count]
+    gram = (product(lin_split, lin_split[0], lin_split[1]) * scale)[:size, :size]
+    lin_out[...] = gram + jnp.where(on[:size, :size], reg_column[:size], 0.0)
+
+    _, reg_column = regs_down(reg_quad)
+
+    def tile(begin, width, kept):
+        feats = [split(col_feats[t, pl.ds(begin, width), :]) for t in range(coords.shape[0])]
+        gram = product(rows_split, jnp.concatenate([f[0] for f in feats], axis=1), jnp.concatenate([f[1] for f in feats], axis=1)) * scale
+        shape = gram.shape
+        on_diag = (lax.broadcasted_iota(jnp.int32, shape, 1) - lax.broadcasted_iota(jnp.int32, shape, 0)
+                   == row_start - col_start - begin)
+        gram += jnp.where(on_diag, reg_column, 0.0)
+        quad_out[:, pl.ds(begin, kept)] = gram[:row_count, :kept]
+
+    whole = col_count // TILE
+
+    @pl.loop(0, whole)
+    def _(n):
+        tile(pl.multiple_of(n * TILE, TILE), TILE, TILE)
+
+    if col_count > whole * TILE:
+        tile(whole * TILE, R, col_count - whole * TILE)
+
+
+def up(value, multiple):
+    return -(-value // multiple) * multiple
+
+
+def gram_call(coords, reg_linear, reg_quadratic, quad_count):
+    chunks, _, width = coords.shape
+    total = chunks * width
+    row_count, col_count = reg_quadratic.shape[0], quad_count // NY
+    size = reg_linear.shape[0]
+    padded = up(row_count, 16)
+    vmem = pl.BlockSpec(memory_space=pltpu.VMEM)
+    f32 = jnp.float32
+    return pl.pallas_call(
+        gram_kernel,
+        out_shape=(
+            jax.ShapeDtypeStruct((R, NC * R), f32),
+            jax.ShapeDtypeStruct((row_count, col_count), f32),
+            jax.ShapeDtypeStruct((size, row_count), f32),
+            jax.ShapeDtypeStruct((size, size), f32),
+        ),
+        in_specs=[vmem] * 3,
+        out_specs=(vmem,) * 4,
+        scratch_shapes=[
+            pltpu.VMEM((chunks, up(row_count, STEP) + STEP, width), f32),
+            pltpu.VMEM((chunks, up(col_count, R) + STEP, width), f32),
+            pltpu.VMEM((2, padded, total), jnp.bfloat16),
+            pltpu.VMEM((2, padded, total), jnp.bfloat16),
+        ],
+        compiler_params=pltpu.CompilerParams(vmem_limit_bytes=48 << 20),
+        name="pair_gram",
+    )(coords, reg_linear.reshape(1, -1), reg_quadratic.reshape(1, -1))
 
 
 def shards(snapshots, basis, reg_linear, reg_quadratic):
-    blocks = gather_call(basis, snapshots).reshape(NC * NY, R, R)
-    every = blocks.transpose(1, 0, 2).reshape(R, NC * NY * R)
-    group = lax.axis_index("snap")
-    local_coords = lax.dynamic_slice_in_dim(every, group * NC * R, NC * R, 1)
-    total = every.shape[1]
-    scale = 1.0 / total
-    row_count = reg_quadratic.shape[0]
-    quad_count = row_count * lax.axis_size("pts")
-    table = jnp.asarray(pair_table(R))
-    row_start = lax.axis_index("pts") * row_count
-    col_count = quad_count // lax.axis_size("snap")
-    col_start = group * col_count
-    row_feats = pair_rows(every, lax.dynamic_slice_in_dim(table, row_start, row_count, 1))
-    col_feats = pair_rows(every, lax.dynamic_slice_in_dim(table, col_start, col_count, 1))
-    block = inner(row_feats, col_feats)
-    row_ids = row_start + jnp.arange(row_count, dtype=jnp.int32)
-    col_ids = col_start + jnp.arange(col_count, dtype=jnp.int32)
-    on_diag = row_ids[:, None] == col_ids[None, :]
-    gram_quad = block * scale + jnp.where(on_diag, reg_quadratic[:, None], 0.0)
-    linear = jnp.concatenate([every, jnp.ones((1, total), jnp.float32)], 0)
-    gram_cross = inner(linear, row_feats) * scale
-    gram_lin = inner(linear, linear) * scale + jnp.diag(reg_linear)
-    return (local_coords, gram_quad, gram_cross, gram_lin)
+    coords = gather_call(basis, snapshots)
+    return gram_call(coords, reg_linear, reg_quadratic, reg_quadratic.shape[0] * NZ * NX * NC)
 
 
 def solution(mesh):

time: 65.4 us -> 39.2 us (0.60)
  local copies, waits for them, and re-layouts: 21.7 us -> 1.59 us
  matrix products: 13.5 us -> 0 us
  Pallas kernels: 29.1 us -> 36.8 us
    gather x4 -> x0, local copies, waits for them, and re-layouts: 17.6 us -> none  [the longest x2 8.86 us: pair_rows(): jnp.take(coords, pairs[0], axis=0) * jnp.take(coords, pairs[1], axis=0)]
    dot_general x3 -> x0, matrix products: 13.5 us -> none  [inner(): lax.dot_general(left, right, (((1,), (1,)), ((), ())), precision=lax.Prec...]
    pallas_call x1 -> x2, Pallas kernels: 29.1 us -> 36.8 us  [the longest x1 29.2 us: gather_call(): pl.pallas_call(gather_kernel, out_shape=jax.ShapeDtypeStruct((NC * NY, R...]
    slice x2 -> x0, local copies, waits for them, and re-layouts: 1.76 us -> none  [pair_rows(): pairs[0]]
    dynamic_slice x1 -> x0, local copies, waits for them, and re-layouts: 0.67 us -> none  [shards(): local_coords = lax.dynamic_slice_in_dim(every, group * NC * R, NC * R, 1)]
    unnamed x4 -> x6, local copies, waits for them, and re-layouts: 1.59 us -> 1.59 us
where the time goes in v2:
time: 39.2 us; the launch traced here: 39.1 us
  Pallas kernels  36.8 us (94%)
  local copies, waits for them, and re-layouts  1.59 us (4%)
  between operations  0.66 us (2%)
    pallas_call x1, Pallas kernels, gather_call(): pl.pallas_call(gather_kernel, out_shape=jax.ShapeDtypeStruct((NC * NY, R...  29.2 us
    pallas_call x1, Pallas kernels, gram_call(): pl.pallas_call(gram_kernel, out_shape=(jax.ShapeDtypeStruct((R, NC * R),...  7.67 us
    unnamed x6, local copies, waits for them, and re-layouts  1.59 us

profile of v2, /device:TPU:1, one launch (start us, length us, event | category | flops | bytes accessed | tf_op | source)
XLA Modules:
  0.0 39.1 jit_solution(14310855464705260471)
XLA Ops:
  0.6 0.0 copy-start
  0.6 1.6 %copy-done = f32[4096,128]{1,0:T(8,128)S(1)} copy-done((f32[4096,128]{1,0:T(8,128)S(1)}, f32[4096,128]{1,0:T(8,128)}, u32[]{:S(2)}) %copy-start) | copy-done | bytes 2097176
  2.2 0.0 copy-start.1
  2.2 0.0 copy-start.2
  2.2 29.2 %project_and_gather.1.coords = f32[8,144,128]{2,1,0:T(8,128)S(1)} custom-call(f32[4096,128]{1,0:T(8,128)S(1)} %copy-done, f32[4096,256]{1,0:T(8,128)} %snaps_hbm.1), custom_call_target="tpu_custom_call" | custom-call | tf_op jit(solution)/shard_map/project_and_gather/pallas_call | solution.py:128
  31.4 0.0 copy-done.1
  31.4 0.0 copy-done.2
  31.4 7.7 %pair_gram.1 = (f32[128,256]{1,0:T(8,128)}, f32[129,2064]{1,0:T(8,128)}, f32[129,129]{1,0:T(8,128)}, f32[129,129]{1,0:T(8,128)}) custom-call(f32[8,144,128]{2,1,0:T(8,128)S(1)} %project_and_gather.1.coords, f32[1,129]{1,0:T(1,128)S(1)} %bitcast.2, f32[1,129]{1,0:T(1,128)S(1)} %bitcast.3), custom_call_target="tpu_custom_call" | custom-call | tf_op jit(solution)/shard_map/pair_gram/pallas_call | solution.py:257
Async XLA Ops:
  0.6 1.6 %copy-start = (f32[4096,128]{1,0:T(8,128)S(1)}, f32[4096,128]{1,0:T(8,128)}, u32[]{:S(2)}) copy-start(f32[4096,128]{1,0:T(8,128)} %basis_hbm.1) | copy-start | bytes 6291460
  2.2 29.2 %copy-start.1 = (f32[129]{0:T(256)S(1)}, f32[129]{0:T(256)}, u32[]{:S(2)}) copy-start(f32[129]{0:T(256)} %param.6) | copy-start | bytes 1552
  2.2 29.2 %copy-start.2 = (f32[129]{0:T(256)S(1)}, f32[129]{0:T(256)}, u32[]{:S(2)}) copy-start(f32[129]{0:T(256)} %param.7) | copy-start | bytes 1552

commit v3 on v2

--- a/solution.py
+++ b/solution.py
@@ -14,6 +14,11 @@
 TILE = 256
 NZ, NX, NC, NY = 8, 4, 2, 4
 XY = [(dx, dy) for dy in range(NY) for dx in range(NX) if dx or dy]
+XY.sort(key=lambda d: min(d[0], NX - d[0]) + min(d[1], NY - d[1]))
+
+
+def far_first(size):
+    return sorted(range(1, size), key=lambda k: -min(k, size - k))
 
 
 def split(value):
@@ -26,32 +31,40 @@
     return lax.dot_general(left, right, (((0,), (0,)), ((), ())), preferred_element_type=jnp.float32)
 
 
-def gather_kernel(basis_hbm, snaps_hbm, out_hbm, basis, snaps, part, peer, half, from_x, from_z, full,
-                  in_sem, c_send, c_recv, x_send, x_recv, z_send, z_recv, xy_send, xy_recv, f_send, f_recv, out_sem):
+def gather_kernel(basis_hbm, snaps_hbm, out, basis, snaps, part, peer, half, from_x, from_z, block,
+                  in_sem, c_send, c_recv, x_send, x_recv, z_send, z_recv, xy_send, xy_recv, b_send, b_recv,
+                  f_send, f_recv, own_sem):
     pts, y = lax.axis_index("pts"), lax.axis_index("snap")
     z, x, c = pts // (NX * NC), (pts // NC) % NX, pts % NC
+    rows, quarter = basis.shape[1], half.shape[1]
 
     def device(z_of, x_of, c_of, y_of):
         return ((z_of * NX + x_of) * NC + c_of, y_of)
 
     sibling = device(z, x, 1 - c, y)
-    x_peers = [device(z, (x + k) % NX, c, y) for k in range(1, NX)]
+    across = device(z, (x + NX // 2) % NX, 1 - c, (y + NY // 2) % NY)
     z_peers = [device((z + k) % NZ, x, c, y) for k in range(1, NZ)]
     xy_peers = [device(z, (x + dx) % NX, c, (y + dy) % NY) for dx, dy in XY]
-
-    barrier = pltpu.get_barrier_semaphore()
-    greeted = [sibling] + z_peers + xy_peers
-    for peer_id in greeted:
-        pl.semaphore_signal(barrier, inc=1, device_id=peer_id, device_id_type=MESH)
-
-    rows = basis.shape[1]
-    quarter = half.shape[1]
+    sends = []
+
     loads = []
     for k in range(CHUNKS):
         for j, (src, dst) in enumerate(((basis_hbm, basis), (snaps_hbm, snaps))):
             load = pltpu.make_async_copy(src.at[pl.ds(k * rows, rows)], dst.at[k], in_sem.at[k, j])
             load.start()
             loads.append(load)
+
+    barrier = pltpu.get_barrier_semaphore()
+    greeted = [sibling, across] + z_peers + xy_peers
+    for peer_id in greeted:
+        pl.semaphore_signal(barrier, inc=1, device_id=peer_id, device_id_type=MESH)
+
+    def send(src, dst, send_sem, recv_sem, target):
+        copy = pltpu.make_async_remote_copy(src, dst, send_sem, recv_sem, device_id=target, device_id_type=MESH)
+        copy.start()
+        sends.append(copy)
+        return copy
+
     for k in range(CHUNKS):
         loads[2 * k].wait()
         loads[2 * k + 1].wait()
@@ -66,58 +79,47 @@
                 part[h] += term[:, h * R:(h + 1) * R]
     pl.semaphore_wait(barrier, len(greeted))
 
-    copy = pltpu.make_async_remote_copy(part.at[1 - c], peer, c_send, c_recv, device_id=sibling, device_id_type=MESH)
-    copy.start()
-    copy.wait()
+    send(part.at[1 - c], peer, c_send, c_recv, sibling).wait_recv()
     half[...] = (part[c] + peer[...]).reshape(half.shape)
 
-    copies = []
-    for k in range(1, NX):
-        copy = pltpu.make_async_remote_copy(half.at[(x + k) % NX], from_x.at[k - 1], x_send.at[k - 1], x_recv.at[k - 1],
-                                            device_id=x_peers[k - 1], device_id_type=MESH)
-        copy.start()
-        copies.append(copy)
+    copies = [send(half.at[(x + k) % NX], from_x.at[k - 1], x_send.at[k - 1], x_recv.at[k - 1],
+                   device(z, (x + k) % NX, c, y)) for k in far_first(NX)]
     for copy in copies:
-        copy.wait()
+        copy.wait_recv()
     from_z[z] = half[x] + from_x[0] + from_x[1] + from_x[2]
 
-    copies = []
-    for k in range(1, NZ):
-        copy = pltpu.make_async_remote_copy(from_z.at[z], from_z.at[z], z_send.at[k - 1], z_recv.at[k - 1],
-                                            device_id=z_peers[k - 1], device_id_type=MESH)
-        copy.start()
-        copies.append(copy)
+    copies = [send(from_z.at[z], from_z.at[z], z_send.at[k - 1], z_recv.at[k - 1], z_peers[k - 1]) for k in far_first(NZ)]
     for copy in copies:
-        copy.wait()
+        copy.wait_recv()
     total = from_z[0]
     for k in range(1, NZ):
         total += from_z[k]
-    mine = full.at[2 * y + c, pl.ds(pl.multiple_of(x * quarter, quarter), quarter)]
-    mine[...] = total
-
-    copies = []
-    for n, peer_id in enumerate(xy_peers):
-        copy = pltpu.make_async_remote_copy(mine, mine, xy_send.at[n], xy_recv.at[n],
-                                            device_id=peer_id, device_id_type=MESH)
-        copy.start()
-        copies.append(copy)
-    handed = []
-    for dy in range(NY):
-        for n, (_, step) in enumerate(XY):
-            if step == dy:
-                copies[n].wait_recv()
-        y_from = (y - dy + NY) % NY
-        copy = pltpu.make_async_remote_copy(full.at[2 * y_from + c], full.at[2 * y_from + c], f_send.at[dy], f_recv.at[dy],
-                                            device_id=sibling, device_id_type=MESH)
-        copy.start()
-        handed.append(copy)
+    block[...] = total
+
+    def place(x_of, y_of):
+        return out.at[NC * y_of + c, pl.ds(pl.multiple_of(x_of * quarter, quarter), quarter)]
+
+    mine = place(x, y)
+    far = len(XY) - 1
+    copies = {far: send(block, mine, xy_send.at[far], xy_recv.at[far], xy_peers[far])}
+    both_cores = send(block, mine, b_send, b_recv, across)
+    for n in range(far - 1, -1, -1):
+        copies[n] = send(block, mine, xy_send.at[n], xy_recv.at[n], xy_peers[n])
+    handed = [send(block, mine, f_send.at[far], f_recv.at[far], sibling)]
+    own = pltpu.make_async_copy(block, mine, own_sem)
+    own.start()
+    for n in range(far):
+        copies[n].wait_recv()
+        dx, dy = XY[n]
+        came = place((x - dx + NX) % NX, (y - dy + NY) % NY)
+        handed.append(send(came, came, f_send.at[n], f_recv.at[n], sibling))
+    copies[far].wait_recv()
+    both_cores.wait_recv()
     for copy in handed:
         copy.wait_recv()
-    copy = pltpu.make_async_copy(full, out_hbm.at[:, pl.ds(0, R)], out_sem)
-    copy.start()
-    for copy_out in copies + handed:
-        copy_out.wait_send()
-    copy.wait()
+    for copy in sends:
+        copy.wait_send()
+    own.wait()
 
 
 def gather_call(basis, snapshots):
@@ -138,16 +140,17 @@
             pltpu.VMEM(block, jnp.float32),
             pltpu.VMEM((NX - 1,) + block[1:], jnp.float32),
             pltpu.VMEM((NZ,) + block[1:], jnp.float32),
-            pltpu.VMEM((NC * NY, R, R), jnp.float32),
+            pltpu.VMEM(block[1:], jnp.float32),
             dma((CHUNKS, 2)),
             dma, dma,
             dma((NX - 1,)), dma((NX - 1,)),
             dma((NZ - 1,)), dma((NZ - 1,)),
             dma((len(XY),)), dma((len(XY),)),
-            dma((NY,)), dma((NY,)),
+            dma, dma,
+            dma((len(XY),)), dma((len(XY),)),
             dma,
         ],
-        compiler_params=pltpu.CompilerParams(collective_id=0, has_side_effects=True, vmem_limit_bytes=48 << 20),
+        compiler_params=pltpu.CompilerParams(collective_id=0, has_side_effects=True, vmem_limit_bytes=52 << 20),
         name="project_and_gather",
     )(basis, snapshots)
 
@@ -234,7 +237,7 @@
 
     whole = col_count // TILE
 
-    @pl.loop(0, whole)
+    @pl.loop(0, whole, unroll=8)
     def _(n):
         tile(pl.multiple_of(n * TILE, TILE), TILE, TILE)
 

time: 39.2 us -> 35.8 us (0.913)
  Pallas kernels: 36.8 us -> 35 us
  local copies, waits for them, and re-layouts: 1.59 us -> 0.01 us
    unnamed x6 -> x4, local copies, waits for them, and re-layouts: 1.59 us -> 0.01 us
    pallas_call x1, Pallas kernels: 7.67 us -> 6.11 us  [gram_call(): pl.pallas_call(gram_kernel, out_shape=(jax.ShapeDtypeStruct((R, NC * R),...]
where the time goes in v3:
time: 35.8 us; the launch traced here: 35.7 us
  Pallas kernels  35 us (98%)
  between operations  0.67 us (2%)
    pallas_call x1, Pallas kernels, gather_call(): pl.pallas_call(gather_kernel, out_shape=jax.ShapeDtypeStruct((NC * NY, R...  28.9 us
    pallas_call x1, Pallas kernels, gram_call(): pl.pallas_call(gram_kernel, out_shape=(jax.ShapeDtypeStruct((R, NC * R),...  6.11 us

profile of v3, /device:TPU:1, one launch (start us, length us, event | category | flops | bytes accessed | tf_op | source)
XLA Modules:
  0.0 35.7 jit_solution(6482028282434704816)
XLA Ops:
  0.6 0.0 copy-start
  0.6 0.0 copy-start.1
  0.7 28.9 %project_and_gather.1.coords = f32[8,144,128]{2,1,0:T(8,128)S(1)} custom-call(f32[4096,128]{1,0:T(8,128)} %basis_hbm.1, f32[4096,256]{1,0:T(8,128)} %snaps_hbm.1), custom_call_target="tpu_custom_call" | custom-call | tf_op jit(solution)/shard_map/project_and_gather/pallas_call | solution.py:130
  29.6 0.0 copy-done
  29.6 0.0 copy-done.1
  29.6 6.1 %pair_gram.1 = (f32[128,256]{1,0:T(8,128)}, f32[129,2064]{1,0:T(8,128)}, f32[129,129]{1,0:T(8,128)}, f32[129,129]{1,0:T(8,128)}) custom-call(f32[8,144,128]{2,1,0:T(8,128)S(1)} %project_and_gather.1.coords, f32[1,129]{1,0:T(1,128)S(1)} %bitcast.2, f32[1,129]{1,0:T(1,128)S(1)} %bitcast.3), custom_call_target="tpu_custom_call" | custom-call | tf_op jit(solution)/shard_map/pair_gram/pallas_call | solution.py:260
Async XLA Ops:
  0.6 28.9 %copy-start = (f32[129]{0:T(256)S(1)}, f32[129]{0:T(256)}, u32[]{:S(2)}) copy-start(f32[129]{0:T(256)} %param.6) | copy-start | bytes 1552
  0.6 28.9 %copy-start.1 = (f32[129]{0:T(256)S(1)}, f32[129]{0:T(256)}, u32[]{:S(2)}) copy-start(f32[129]{0:T(256)} %param.7) | copy-start | bytes 1552

commit v4 on v3

--- a/solution.py
+++ b/solution.py
@@ -9,12 +9,18 @@
 
 R = 128
 MESH = pl.DeviceIdType.MESH
-CHUNKS = 8
+CHUNKS = 4
 STEP = 16
 TILE = 256
 NZ, NX, NC, NY = 8, 4, 2, 4
 XY = [(dx, dy) for dy in range(NY) for dx in range(NX) if dx or dy]
-XY.sort(key=lambda d: min(d[0], NX - d[0]) + min(d[1], NY - d[1]))
+
+
+def hops(step):
+    return min(step[0], NX - step[0]) + min(step[1], NY - step[1])
+
+
+XY.sort(key=hops)
 
 
 def far_first(size):
@@ -32,7 +38,7 @@
 
 
 def gather_kernel(basis_hbm, snaps_hbm, out, basis, snaps, part, peer, half, from_x, from_z, block,
-                  in_sem, c_send, c_recv, x_send, x_recv, z_send, z_recv, xy_send, xy_recv, b_send, b_recv,
+                  in_sem, c_send, c_recv, x_send, x_recv, z_send, z_recv, xy_send, xy_recv,
                   f_send, f_recv, own_sem):
     pts, y = lax.axis_index("pts"), lax.axis_index("snap")
     z, x, c = pts // (NX * NC), (pts // NC) % NX, pts % NC
@@ -42,7 +48,6 @@
         return ((z_of * NX + x_of) * NC + c_of, y_of)
 
     sibling = device(z, x, 1 - c, y)
-    across = device(z, (x + NX // 2) % NX, 1 - c, (y + NY // 2) % NY)
     z_peers = [device((z + k) % NZ, x, c, y) for k in range(1, NZ)]
     xy_peers = [device(z, (x + dx) % NX, c, (y + dy) % NY) for dx, dy in XY]
     sends = []
@@ -55,7 +60,7 @@
             loads.append(load)
 
     barrier = pltpu.get_barrier_semaphore()
-    greeted = [sibling, across] + z_peers + xy_peers
+    greeted = [sibling] + z_peers + xy_peers
     for peer_id in greeted:
         pl.semaphore_signal(barrier, inc=1, device_id=peer_id, device_id_type=MESH)
 
@@ -100,21 +105,18 @@
         return out.at[NC * y_of + c, pl.ds(pl.multiple_of(x_of * quarter, quarter), quarter)]
 
     mine = place(x, y)
-    far = len(XY) - 1
-    copies = {far: send(block, mine, xy_send.at[far], xy_recv.at[far], xy_peers[far])}
-    both_cores = send(block, mine, b_send, b_recv, across)
-    for n in range(far - 1, -1, -1):
+    last = len(XY)
+    copies, handed = {}, []
+    for n in range(last - 1, -1, -1):
         copies[n] = send(block, mine, xy_send.at[n], xy_recv.at[n], xy_peers[n])
-    handed = [send(block, mine, f_send.at[far], f_recv.at[far], sibling)]
+    handed.append(send(block, mine, f_send.at[last], f_recv.at[last], sibling))
     own = pltpu.make_async_copy(block, mine, own_sem)
     own.start()
-    for n in range(far):
+    for n in range(last):
         copies[n].wait_recv()
         dx, dy = XY[n]
         came = place((x - dx + NX) % NX, (y - dy + NY) % NY)
         handed.append(send(came, came, f_send.at[n], f_recv.at[n], sibling))
-    copies[far].wait_recv()
-    both_cores.wait_recv()
     for copy in handed:
         copy.wait_recv()
     for copy in sends:
@@ -146,8 +148,7 @@
             dma((NX - 1,)), dma((NX - 1,)),
             dma((NZ - 1,)), dma((NZ - 1,)),
             dma((len(XY),)), dma((len(XY),)),
-            dma, dma,
-            dma((len(XY),)), dma((len(XY),)),
+            dma((len(XY) + 1,)), dma((len(XY) + 1,)),
             dma,
         ],
         compiler_params=pltpu.CompilerParams(collective_id=0, has_side_effects=True, vmem_limit_bytes=52 << 20),

time: 35.8 us -> 35.1 us (0.980)
  Pallas kernels: 35 us -> 34.3 us
    pallas_call x1, Pallas kernels: 28.9 us -> 28.2 us  [gather_call(): pl.pallas_call(gather_kernel, out_shape=jax.ShapeDtypeStruct((NC * NY, R...]
where the time goes in v4:
time: 35.1 us; the launch traced here: 35 us
  Pallas kernels  34.3 us (98%)
  between operations  0.67 us (2%)
    pallas_call x1, Pallas kernels, gather_call(): pl.pallas_call(gather_kernel, out_shape=jax.ShapeDtypeStruct((NC * NY, R...  28.2 us
    pallas_call x1, Pallas kernels, gram_call(): pl.pallas_call(gram_kernel, out_shape=(jax.ShapeDtypeStruct((R, NC * R),...  6.11 us

profile of v4, /device:TPU:1, one launch (start us, length us, event | category | flops | bytes accessed | tf_op | source)
XLA Modules:
  0.0 35.0 jit_solution(12081387679978537229)
XLA Ops:
  0.6 0.0 copy-start
  0.6 0.0 copy-start.1
  0.7 28.2 %project_and_gather.1.coords = f32[8,144,128]{2,1,0:T(8,128)S(1)} custom-call(f32[4096,128]{1,0:T(8,128)} %basis_hbm.1, f32[4096,256]{1,0:T(8,128)} %snaps_hbm.1), custom_call_target="tpu_custom_call" | custom-call | tf_op jit(solution)/shard_map/project_and_gather/pallas_call | solution.py:132
  28.9 0.0 copy-done
  28.9 0.0 copy-done.1
  28.9 6.1 %pair_gram.1 = (f32[128,256]{1,0:T(8,128)}, f32[129,2064]{1,0:T(8,128)}, f32[129,129]{1,0:T(8,128)}, f32[129,129]{1,0:T(8,128)}) custom-call(f32[8,144,128]{2,1,0:T(8,128)S(1)} %project_and_gather.1.coords, f32[1,129]{1,0:T(1,128)S(1)} %bitcast.2, f32[1,129]{1,0:T(1,128)S(1)} %bitcast.3), custom_call_target="tpu_custom_call" | custom-call | tf_op jit(solution)/shard_map/pair_gram/pallas_call | solution.py:261
Async XLA Ops:
  0.6 28.3 %copy-start = (f32[129]{0:T(256)S(1)}, f32[129]{0:T(256)}, u32[]{:S(2)}) copy-start(f32[129]{0:T(256)} %param.6) | copy-start | bytes 1552
  0.6 28.3 %copy-start.1 = (f32[129]{0:T(256)S(1)}, f32[129]{0:T(256)}, u32[]{:S(2)}) copy-start(f32[129]{0:T(256)} %param.7) | copy-start | bytes 1552

commit v5 on v4

--- a/solution.py
+++ b/solution.py
@@ -21,6 +21,7 @@
 
 
 XY.sort(key=hops)
+ROW = [(dx, dc) for dx in (2, 1, 3, 0) for dc in range(NC) if dx or dc]
 
 
 def far_first(size):
@@ -37,12 +38,12 @@
     return lax.dot_general(left, right, (((0,), (0,)), ((), ())), preferred_element_type=jnp.float32)
 
 
-def gather_kernel(basis_hbm, snaps_hbm, out, basis, snaps, part, peer, half, from_x, from_z, block,
-                  in_sem, c_send, c_recv, x_send, x_recv, z_send, z_recv, xy_send, xy_recv,
+def gather_kernel(basis_hbm, snaps_hbm, out, basis, snaps, part, from_x, from_z, block,
+                  in_sem, x_send, x_recv, z_send, z_recv, xy_send, xy_recv,
                   f_send, f_recv, own_sem):
     pts, y = lax.axis_index("pts"), lax.axis_index("snap")
     z, x, c = pts // (NX * NC), (pts // NC) % NX, pts % NC
-    rows, quarter = basis.shape[1], half.shape[1]
+    rows, quarter = basis.shape[1], part.shape[2]
 
     def device(z_of, x_of, c_of, y_of):
         return ((z_of * NX + x_of) * NC + c_of, y_of)
@@ -50,6 +51,7 @@
     sibling = device(z, x, 1 - c, y)
     z_peers = [device((z + k) % NZ, x, c, y) for k in range(1, NZ)]
     xy_peers = [device(z, (x + dx) % NX, c, (y + dy) % NY) for dx, dy in XY]
+    row_peers = [device(z, (x + dx) % NX, (c + dc) % NC, y) for dx, dc in ROW]
     sends = []
 
     loads = []
@@ -60,7 +62,7 @@
             loads.append(load)
 
     barrier = pltpu.get_barrier_semaphore()
-    greeted = [sibling] + z_peers + xy_peers
+    greeted = [peer for peer, (_, dc) in zip(row_peers, ROW) if dc] + z_peers + xy_peers
     for peer_id in greeted:
         pl.semaphore_signal(barrier, inc=1, device_id=peer_id, device_id_type=MESH)
 
@@ -79,19 +81,19 @@
         term = both[:R] + both[R:] + dot_rows(b_high, s_low)
         for h in range(NC):
             if k == 0:
-                part[h] = term[:, h * R:(h + 1) * R]
+                part[h] = term[:, h * R:(h + 1) * R].reshape(part.shape[1:])
             else:
-                part[h] += term[:, h * R:(h + 1) * R]
+                part[h] += term[:, h * R:(h + 1) * R].reshape(part.shape[1:])
     pl.semaphore_wait(barrier, len(greeted))
 
-    send(part.at[1 - c], peer, c_send, c_recv, sibling).wait_recv()
-    half[...] = (part[c] + peer[...]).reshape(half.shape)
-
-    copies = [send(half.at[(x + k) % NX], from_x.at[k - 1], x_send.at[k - 1], x_recv.at[k - 1],
-                   device(z, (x + k) % NX, c, y)) for k in far_first(NX)]
+    copies = [send(part.at[(c + dc) % NC, (x + dx) % NX], from_x.at[n], x_send.at[n], x_recv.at[n], row_peers[n])
+              for n, (dx, dc) in enumerate(ROW)]
     for copy in copies:
         copy.wait_recv()
-    from_z[z] = half[x] + from_x[0] + from_x[1] + from_x[2]
+    total = part[c, x]
+    for n in range(len(ROW)):
+        total += from_x[n]
+    from_z[z] = total
 
     copies = [send(from_z.at[z], from_z.at[z], z_send.at[k - 1], z_recv.at[k - 1], z_peers[k - 1]) for k in far_first(NZ)]
     for copy in copies:
@@ -137,15 +139,12 @@
         scratch_shapes=[
             pltpu.VMEM((CHUNKS, rows, R), jnp.float32),
             pltpu.VMEM((CHUNKS, rows, width), jnp.float32),
-            pltpu.VMEM((NC, R, R), jnp.float32),
-            pltpu.VMEM((R, R), jnp.float32),
-            pltpu.VMEM(block, jnp.float32),
-            pltpu.VMEM((NX - 1,) + block[1:], jnp.float32),
+            pltpu.VMEM((NC,) + block, jnp.float32),
+            pltpu.VMEM((len(ROW),) + block[1:], jnp.float32),
             pltpu.VMEM((NZ,) + block[1:], jnp.float32),
             pltpu.VMEM(block[1:], jnp.float32),
             dma((CHUNKS, 2)),
-            dma, dma,
-            dma((NX - 1,)), dma((NX - 1,)),
+            dma((len(ROW),)), dma((len(ROW),)),
             dma((NZ - 1,)), dma((NZ - 1,)),
             dma((len(XY),)), dma((len(XY),)),
             dma((len(XY) + 1,)), dma((len(XY) + 1,)),

time: 35.1 us -> 34.5 us (0.983)
  Pallas kernels: 34.3 us -> 33.8 us
    pallas_call x1, Pallas kernels: 28.2 us -> 27.6 us  [gather_call(): pl.pallas_call(gather_kernel, out_shape=jax.ShapeDtypeStruct((NC * NY, R...]
where the time goes in v5:
time: 34.5 us; the launch traced here: 34.4 us
  Pallas kernels  33.8 us (98%)
  between operations  0.67 us (2%)
    pallas_call x1, Pallas kernels, gather_call(): pl.pallas_call(gather_kernel, out_shape=jax.ShapeDtypeStruct((NC * NY, R...  27.6 us
    pallas_call x1, Pallas kernels, gram_call(): pl.pallas_call(gram_kernel, out_shape=(jax.ShapeDtypeStruct((R, NC * R),...  6.11 us

profile of v5, /device:TPU:1, one launch (start us, length us, event | category | flops | bytes accessed | tf_op | source)
XLA Modules:
  0.0 34.4 jit_solution(14670970765810818115)
XLA Ops:
  0.6 0.0 copy-start
  0.6 0.0 copy-start.1
  0.7 27.6 %project_and_gather.1.coords = f32[8,144,128]{2,1,0:T(8,128)S(1)} custom-call(f32[4096,128]{1,0:T(8,128)} %basis_hbm.1, f32[4096,256]{1,0:T(8,128)} %snaps_hbm.1), custom_call_target="tpu_custom_call" | custom-call | tf_op jit(solution)/shard_map/project_and_gather/pallas_call | solution.py:134
  28.3 0.0 copy-done
  28.3 0.0 copy-done.1
  28.3 6.1 %pair_gram.1 = (f32[128,256]{1,0:T(8,128)}, f32[129,2064]{1,0:T(8,128)}, f32[129,129]{1,0:T(8,128)}, f32[129,129]{1,0:T(8,128)}) custom-call(f32[8,144,128]{2,1,0:T(8,128)S(1)} %project_and_gather.1.coords, f32[1,129]{1,0:T(1,128)S(1)} %bitcast.2, f32[1,129]{1,0:T(1,128)S(1)} %bitcast.3), custom_call_target="tpu_custom_call" | custom-call | tf_op jit(solution)/shard_map/pair_gram/pallas_call | solution.py:260
Async XLA Ops:
  0.6 27.7 %copy-start = (f32[129]{0:T(256)S(1)}, f32[129]{0:T(256)}, u32[]{:S(2)}) copy-start(f32[129]{0:T(256)} %param.6) | copy-start | bytes 1552
  0.6 27.7 %copy-start.1 = (f32[129]{0:T(256)S(1)}, f32[129]{0:T(256)}, u32[]{:S(2)}) copy-start(f32[129]{0:T(256)} %param.7) | copy-start | bytes 1552

commit v6 on v5

--- a/solution.py
+++ b/solution.py
@@ -21,7 +21,7 @@
 
 
 XY.sort(key=hops)
-ROW = [(dx, dc) for dx in (2, 1, 3, 0) for dc in range(NC) if dx or dc]
+ROW = [(dx, dc) for dx in (0, 2, 1, 3) for dc in range(NC) if dx or dc]
 
 
 def far_first(size):
@@ -109,9 +109,9 @@
     mine = place(x, y)
     last = len(XY)
     copies, handed = {}, []
+    handed.append(send(block, mine, f_send.at[last], f_recv.at[last], sibling))
     for n in range(last - 1, -1, -1):
         copies[n] = send(block, mine, xy_send.at[n], xy_recv.at[n], xy_peers[n])
-    handed.append(send(block, mine, f_send.at[last], f_recv.at[last], sibling))
     own = pltpu.make_async_copy(block, mine, own_sem)
     own.start()
     for n in range(last):

time: 34.5 us -> 34.5 us (level)
  no operation moved by 1% of the time
where the time goes in v6:
time: 34.5 us; the launch traced here: 34.4 us
  Pallas kernels  33.8 us (98%)
  between operations  0.67 us (2%)
    pallas_call x1, Pallas kernels, gather_call(): pl.pallas_call(gather_kernel, out_shape=jax.ShapeDtypeStruct((NC * NY, R...  27.7 us
    pallas_call x1, Pallas kernels, gram_call(): pl.pallas_call(gram_kernel, out_shape=(jax.ShapeDtypeStruct((R, NC * R),...  6.11 us

profile of v6, /device:TPU:1, one launch (start us, length us, event | category | flops | bytes accessed | tf_op | source)
XLA Modules:
  0.0 34.4 jit_solution(16611834061770637871)
XLA Ops:
  0.6 0.0 copy-start
  0.6 0.0 copy-start.1
  0.7 27.7 %project_and_gather.1.coords = f32[8,144,128]{2,1,0:T(8,128)S(1)} custom-call(f32[4096,128]{1,0:T(8,128)} %basis_hbm.1, f32[4096,256]{1,0:T(8,128)} %snaps_hbm.1), custom_call_target="tpu_custom_call" | custom-call | tf_op jit(solution)/shard_map/project_and_gather/pallas_call | solution.py:134
  28.3 0.0 copy-done
  28.3 0.0 copy-done.1
  28.3 6.1 %pair_gram.1 = (f32[128,256]{1,0:T(8,128)}, f32[129,2064]{1,0:T(8,128)}, f32[129,129]{1,0:T(8,128)}, f32[129,129]{1,0:T(8,128)}) custom-call(f32[8,144,128]{2,1,0:T(8,128)S(1)} %project_and_gather.1.coords, f32[1,129]{1,0:T(1,128)S(1)} %bitcast.2, f32[1,129]{1,0:T(1,128)S(1)} %bitcast.3), custom_call_target="tpu_custom_call" | custom-call | tf_op jit(solution)/shard_map/pair_gram/pallas_call | solution.py:260
Async XLA Ops:
  0.6 27.7 %copy-start = (f32[129]{0:T(256)S(1)}, f32[129]{0:T(256)}, u32[]{:S(2)}) copy-start(f32[129]{0:T(256)} %param.6) | copy-start | bytes 1552
  0.6 27.7 %copy-start.1 = (f32[129]{0:T(256)S(1)}, f32[129]{0:T(256)}, u32[]{:S(2)}) copy-start(f32[129]{0:T(256)} %param.7) | copy-start | bytes 1552

commit v7 on v6

--- a/solution.py
+++ b/solution.py
@@ -9,7 +9,7 @@
 
 R = 128
 MESH = pl.DeviceIdType.MESH
-CHUNKS = 4
+CHUNKS = (1280, 1280, 1024, 512)
 STEP = 16
 TILE = 256
 NZ, NX, NC, NY = 8, 4, 2, 4
@@ -43,7 +43,9 @@
                   f_send, f_recv, own_sem):
     pts, y = lax.axis_index("pts"), lax.axis_index("snap")
     z, x, c = pts // (NX * NC), (pts // NC) % NX, pts % NC
-    rows, quarter = basis.shape[1], part.shape[2]
+    quarter = part.shape[2]
+    ends = [sum(CHUNKS[:k + 1]) for k in range(len(CHUNKS))]
+    spans = [pl.ds(end - rows, rows) for end, rows in zip(ends, CHUNKS)]
 
     def device(z_of, x_of, c_of, y_of):
         return ((z_of * NX + x_of) * NC + c_of, y_of)
@@ -55,9 +57,9 @@
     sends = []
 
     loads = []
-    for k in range(CHUNKS):
+    for k, span in enumerate(spans):
         for j, (src, dst) in enumerate(((basis_hbm, basis), (snaps_hbm, snaps))):
-            load = pltpu.make_async_copy(src.at[pl.ds(k * rows, rows)], dst.at[k], in_sem.at[k, j])
+            load = pltpu.make_async_copy(src.at[span], dst.at[span], in_sem.at[k, j])
             load.start()
             loads.append(load)
 
@@ -72,11 +74,11 @@
         sends.append(copy)
         return copy
 
-    for k in range(CHUNKS):
+    for k, span in enumerate(spans):
         loads[2 * k].wait()
         loads[2 * k + 1].wait()
-        b_high, b_low = split(basis[k])
-        s_high, s_low = split(snaps[k])
+        b_high, b_low = split(basis[span])
+        s_high, s_low = split(snaps[span])
         both = dot_rows(jnp.concatenate([b_high, b_low], axis=1), s_high)
         term = both[:R] + both[R:] + dot_rows(b_high, s_low)
         for h in range(NC):
@@ -128,7 +130,6 @@
 
 def gather_call(basis, snapshots):
     points, width = snapshots.shape
-    rows = points // CHUNKS
     dma = pltpu.SemaphoreType.DMA
     block = (NX, R // NX, R)
     return pl.pallas_call(
@@ -137,13 +138,13 @@
         in_specs=[pl.BlockSpec(memory_space=pl.ANY)] * 2,
         out_specs=pl.BlockSpec(memory_space=pl.ANY),
         scratch_shapes=[
-            pltpu.VMEM((CHUNKS, rows, R), jnp.float32),
-            pltpu.VMEM((CHUNKS, rows, width), jnp.float32),
+            pltpu.VMEM((points, R), jnp.float32),
+            pltpu.VMEM((points, width), jnp.float32),
             pltpu.VMEM((NC,) + block, jnp.float32),
             pltpu.VMEM((len(ROW),) + block[1:], jnp.float32),
             pltpu.VMEM((NZ,) + block[1:], jnp.float32),
             pltpu.VMEM(block[1:], jnp.float32),
-            dma((CHUNKS, 2)),
+            dma((len(CHUNKS), 2)),
             dma((len(ROW),)), dma((len(ROW),)),
             dma((NZ - 1,)), dma((NZ - 1,)),
             dma((len(XY),)), dma((len(XY),)),

time: 34.5 us -> 34.5 us (level)
  no operation moved by 1% of the time
where the time goes in v7:
time: 34.5 us; the launch traced here: 34.4 us
  Pallas kernels  33.8 us (98%)
  between operations  0.67 us (2%)
    pallas_call x1, Pallas kernels, gather_call(): pl.pallas_call(gather_kernel, out_shape=jax.ShapeDtypeStruct((NC * NY, R...  27.7 us
    pallas_call x1, Pallas kernels, gram_call(): pl.pallas_call(gram_kernel, out_shape=(jax.ShapeDtypeStruct((R, NC * R),...  6.11 us

profile of v7, /device:TPU:1, one launch (start us, length us, event | category | flops | bytes accessed | tf_op | source)
XLA Modules:
  0.0 34.4 jit_solution(2040635645936345999)
XLA Ops:
  0.6 0.0 copy-start
  0.6 0.0 copy-start.1
  0.7 27.7 %project_and_gather.1.coords = f32[8,144,128]{2,1,0:T(8,128)S(1)} custom-call(f32[4096,128]{1,0:T(8,128)} %basis_hbm.1, f32[4096,256]{1,0:T(8,128)} %snaps_hbm.1), custom_call_target="tpu_custom_call" | custom-call | tf_op jit(solution)/shard_map/project_and_gather/pallas_call | solution.py:135
  28.3 0.0 copy-done
  28.3 0.0 copy-done.1
  28.3 6.1 %pair_gram.1 = (f32[128,256]{1,0:T(8,128)}, f32[129,2064]{1,0:T(8,128)}, f32[129,129]{1,0:T(8,128)}, f32[129,129]{1,0:T(8,128)}) custom-call(f32[8,144,128]{2,1,0:T(8,128)S(1)} %project_and_gather.1.coords, f32[1,129]{1,0:T(1,128)S(1)} %bitcast.2, f32[1,129]{1,0:T(1,128)S(1)} %bitcast.3), custom_call_target="tpu_custom_call" | custom-call | tf_op jit(solution)/shard_map/pair_gram/pallas_call | solution.py:261
Async XLA Ops:
  0.6 27.7 %copy-start = (f32[129]{0:T(256)S(1)}, f32[129]{0:T(256)}, u32[]{:S(2)}) copy-start(f32[129]{0:T(256)} %param.6) | copy-start | bytes 1552
  0.6 27.7 %copy-start.1 = (f32[129]{0:T(256)S(1)}, f32[129]{0:T(256)}, u32[]{:S(2)}) copy-start(f32[129]{0:T(256)} %param.7) | copy-start | bytes 1552
